TPU v7x, 32 devices: a whole 2x2x4 slice. The times are simulated.
32 devices in a mesh: grp: 4 (over z), tile: 4 (over y, core), rep: 2 (over x).
Axes of the slice: x: 2, y: 2, z: 4, core: 2. Of those that a mesh axis runs over, the one named last changes fastest.
Arguments:
- amplitudes: bfloat16 [64, 8, 4096], P(('grp', 'tile')), may hold values from -6 to 6
- tile_blocks: int32 [64, 2], P(('grp', 'tile')), may hold values from 0 to 63, as said below
- live_rows: int32 [64], P(('grp', 'tile')), may hold values from 4 to 8
- ladder_factors: bfloat16 [32, 2, 32, 4096], P('tile', None, 'rep'), may hold values from -0.3125 to 0.3125
- cycle_coupling: bfloat16 [64, 8, 8], replicated, may hold values from -2 to 2
- block_owner: int32 [32], replicated, may hold values from 0 to 31, as said below
Outputs:
- residual: bfloat16 [64, 8, 4096], P(('grp', 'tile'), 'rep')
Inputs may be any that keep to these rules, and one draw needn't show every extreme that they name: Column 0 is an occupied-pair block below 64, column 1 a virtual-pair block below 32. Among the tiles of one index pair of grp and tile, at most 2 have blocks whose owner position block_owner[tile_blocks[k, 1]] // 8 is the same; in every group of grp some owner has exactly 2 from every index of tile. `block_owner`: A permutation of the virtual-pair blocks.
All inputs are finite; a program needn't handle non-finite values.
Results may differ from a plain program's by a relative error of at most 0.0036.
Values may be sent and summed in bfloat16 or wider, within the bound.
A program may use at most 64 MiB of HBM per device.

v0:
```python
import jax
import jax.numpy as jnp
from jax import lax
from jax.sharding import PartitionSpec as P

VB = 64
CAP = 2


def aux_group(total, load):
    group = max(1, 512 // max(load, 1))
    group = min(group, total)
    for trial in range(group, 0, -1):
        return trial
    return 1


def ladder_block(buffer, labels, factors):
    count = buffer.shape[0]
    rows = buffer.shape[1]
    depth = factors.shape[2]
    index = labels.astype(jnp.int32)
    grid = buffer.reshape(count, rows, VB, VB)
    group = aux_group(depth, count * rows)

    def step(total, start):
        portion = lax.dynamic_slice_in_dim(factors, start * group, group, 2)
        picked = jnp.take(portion, index, axis=0).reshape(count, 2, group, VB, VB)
        middle = jnp.einsum(
            "kqac,kpcd->kpqad", picked[:, 0], grid, preferred_element_type=jnp.float32
        ).astype(jnp.bfloat16)
        total = total + jnp.einsum(
            "kpqad,kqbd->kpab", middle, picked[:, 1], preferred_element_type=jnp.float32
        )
        return (total, None)

    start_total = jnp.zeros((count, rows, VB, VB), jnp.float32)
    total, unused = lax.scan(step, start_total, jnp.arange(depth // group))
    return total.reshape(count, rows, VB * VB)


def send_back(values):
    return lax.all_to_all(values, "tile", split_axis=0, concat_axis=0, tiled=True)


def rep_total(values):
    return lax.psum_scatter(values, "rep", scatter_dimension=1, tiled=True)


def local(amplitudes, tile_blocks, live_rows, ladder_factors, cycle_coupling, block_owner):
    rows = amplitudes.shape[1]
    cells = amplitudes.shape[2]
    peers = lax.axis_size("tile")
    reps = lax.axis_size("rep")
    owned = ladder_factors.shape[0]
    capacity = CAP
    share = rows // reps
    lead = lax.axis_index("rep") * share
    live = jnp.arange(rows)[None, :] < live_rows[:, None]
    masked = jnp.where(live[:, :, None], amplitudes, jnp.zeros_like(amplitudes))
    pick = tile_blocks[:, 1:2] == jnp.arange(block_owner.shape[0])[None, :]
    place = jnp.sum(jnp.where(pick, block_owner[None, :], 0), axis=1)
    target = place // owned
    within = place % owned
    onehot_target = (target[:, None] == jnp.arange(peers)[None, :]).astype(jnp.int32)
    earlier = jnp.cumsum(onehot_target, axis=0) - onehot_target
    rank_own = jnp.sum(earlier * onehot_target, axis=1)
    slot = target * capacity + rank_own
    slots_total = peers * capacity
    spread = (slot[None, :] == jnp.arange(slots_total)[:, None]).astype(jnp.bfloat16)
    chosen = (tile_blocks[:, 0:1] == jnp.arange(cycle_coupling.shape[0])[None, :]).astype(
        jnp.bfloat16
    )
    coupling = jnp.einsum(
        "kn,npq->kpq", chosen, cycle_coupling, preferred_element_type=jnp.float32
    ).astype(jnp.bfloat16)
    coupling_rows = lax.dynamic_slice_in_dim(coupling, lead, share, 1)
    cycle = jnp.einsum("kpq,kqx->kpx", coupling_rows, masked, preferred_element_type=jnp.float32)
    width = masked.shape[1]
    packed = jnp.einsum("sk,krx->srx", spread, masked, preferred_element_type=jnp.float32).astype(
        jnp.bfloat16
    )
    packed = packed.reshape(peers, capacity, width, cells)
    labels = jnp.sum(spread.astype(jnp.float32) * within[None, :].astype(jnp.float32), axis=1)
    labels = labels.astype(jnp.bfloat16).reshape(peers, capacity)
    buffer = lax.all_to_all(packed, "tile", split_axis=0, concat_axis=0, tiled=True)
    tags = lax.all_to_all(labels, "tile", split_axis=0, concat_axis=0, tiled=True)
    sources = buffer.shape[0]
    slots = buffer.shape[1]
    terms = ladder_block(
        buffer.reshape(sources * slots, width, cells), tags.reshape(sources * slots), ladder_factors
    )
    partial_value = terms.reshape(sources, slots, width, cells)
    returned = send_back(partial_value)
    mine = jnp.take(returned.reshape(slots_total, width, cells), slot, axis=0)
    ladder_rows = rep_total(mine)
    return (ladder_rows + cycle).astype(jnp.bfloat16)


def solution(mesh):
    placed = (
        P(("grp", "tile"), None, None),
        P(("grp", "tile"), None),
        P(("grp", "tile")),
        P("tile", None, "rep", None),
        P(),
        P(),
    )
    return jax.shard_map(
        local,
        mesh=mesh,
        in_specs=placed,
        out_specs=P(("grp", "tile"), "rep", None),
        check_vma=False,
    )
```

profile of v0, /device:TPU:0, one launch (start us, length us, event | category | flops | bytes accessed | tf_op | source)
XLA Modules:
  0.0 122.5 jit_solution(6654075669870718299)
XLA Ops:
  6.5 0.0 copy-start
  6.5 0.8 slice_bitcast_fusion.5
  7.3 0.8 select_reduce_fusion.1
  8.1 0.1 fusion.15
  8.3 0.2 select_reduce_fusion
  8.5 0.1 multiply_reduce_fusion
  8.5 0.7 convert_element_type.67
  9.2 4.2 %all-to-all-start = ((bf16[4,1,2]{2,1,0:T(2,128)(2,1)}), bf16[4,1,2]{2,1,0:T(2,128)(2,1)S(1)}, u32[]{:S(2)}, u32[]{:S(2)}) async-start(bf16[4,1,2]{2,1,0:T(2,128)(2,1)} %convert_element_type.67), calls=%async_computation | async-start | bytes 4096 | tf_op jit(solution)/shard_map/all_to_all | solution.py:87
  13.5 0.7 iota_compare_fusion.1
  14.2 1.0 broadcast_select_fusion.2
  15.2 0.4 convolution_convert_fusion
  15.7 0.3 reshape.183
  16.0 1.3 %copy.27 = bf16[4,2,8,4096]{3,1,2,0:T(2,128)(2,1)} copy(bf16[4,2,8,4096]{3,1,0,2:T(2,128)(2,1)S(1)} %reshape.183) | data formatting | bytes 1048576 | tf_op jit(solution)/shard_map/reshape | solution.py:83
  17.3 0.0 all-to-all-done
  17.3 3.5 %all-to-all-start.1 = ((bf16[4,2,8,4096]{3,1,2,0:T(2,128)(2,1)}), bf16[4,2,8,4096]{3,1,2,0:T(2,128)(2,1)S(1)}, u32[]{:S(2)}, u32[]{:S(2)}) async-start(bf16[4,2,8,4096]{3,1,2,0:T(2,128)(2,1)} %copy.27), calls=%async_computation.1 | async-start | bytes 1048576 | tf_op jit(solution)/shard_map/all_to_all | solution.py:86
  20.8 0.1 reshape.185
  20.9 8.7 %all-to-all-done.1 = bf16[4,2,8,4096]{3,1,2,0:T(2,128)(2,1)S(1)} async-done(((bf16[4,2,8,4096]{3,1,2,0:T(2,128)(2,1)}), bf16[4,2,8,4096]{3,1,2,0:T(2,128)(2,1)S(1)}, u32[]{:S(2)}, u32[]{:S(2)}) %all-to-all-start.1) | async-done | bytes 524320 | tf_op jit(solution)/shard_map/all_to_all | solution.py:86
  29.6 0.3 copy.28
  29.9 2.1 %reshape_reshape.6 = bf16[8,8,64,64]{3,2,1,0:T(8,128)(2,1)} reshape(bf16[4,2,8,4096]{3,2,1,0:T(8,128)(2,1)S(1)} %copy.28) | data formatting | bytes 1048576 | tf_op jit(solution)/shard_map/reshape;reshape | solution.py:23
  32.0 29.8 %while.11 = (s32[]{:T(128)}, f32[8,8,64,64]{3,2,1,0:T(8,128)}, s32[8]{0:T(128)S(1)}, s32[2]{0:T(128)S(1)}, bf16[8,2,16,4096]{3,2,1,0:T(8,128)(2,1)}, /*index=5*/...) while((s32[]{:T(128)}, f32[8,8,64,64]{3,2,1,0:T(8,128)}, ...), condition=%wide.region_5.6_spmd.clone, body=%wide.region_4.5_spmd.clone.sunk | while | flops 540017728 | bytes 16257401 | solution.py:38
  32.0 0.6 dynamic_slice.19
  33.2 1.3 %constant_dynamic-slice_fusion.2 = bf16[8,2,8,4096]{3,2,1,0:T(8,128)(2,1)S(1)} fusion(bf16[8,2,16,4096]{3,2,1,0:T(8,128)(2,1)} %get-tuple-element.138, s32[]{:T(128)S(6)} %select_n.131), kind=kLoop, calls=%fused_computation.16.clone.1 | loop fusion | bytes 2097156 | tf_op jit(solution)/shard_map/while/body/eval_jaxpr/dynamic_slice | solution.py:27
  34.5 0.6 gather_fusion
  35.1 0.1 copy.41
  35.2 2.3 %gather.20 = bf16[8,2,8,64,64]{4,3,2,0,1:T(8,128)(2,1)S(1)} reshape(bf16[8,2,8,4096]{3,2,0,1:T(8,128)(2,1)S(1)} %copy.41) | data formatting | bytes 2097152 | tf_op jit(solution)/shard_map/while/body/eval_jaxpr/jit(_take)/gather | solution.py:28
  37.5 0.0 copy-start.1
  37.6 1.6 %broadcast_select_fusion.4 = bf16[8,2,8,64,64]{4,3,2,0,1:T(8,128)(2,1)} fusion(bf16[8,2,8,64,64]{4,3,2,0,1:T(8,128)(2,1)S(1)} %gather.20, pred[8]{0:T(512)(128)(4,1)S(1)} %compare_and_fusion.3), kind=kLoop, calls=%fused_computation.7.clone.1 | loop fusion | flops 524288 | bytes 2097160 | tf_op jit(solution)/shard_map/while/body/eval_jaxpr/jit(_take)/select_n | solution.py:28
  39.1 0.0 copy-done.1
  39.1 7.4 %bitcast_add_fusion.3 = f32[8,8,64,64]{3,2,1,0:T(8,128)} fusion(f32[8,8,64,64]{3,2,1,0:T(8,128)} %get-tuple-element.125, bf16[8,2,8,64,64]{4,3,2,0,1:T(8,128)(2,1)} %broadcast_select_fusion.4, bf16[8,8,64,64]{3,2,1,0:T(8,128)(2,1)S(1)} %copy-done.1, pred[]{:T(512)S(6)} %compare.30), kind=kOutput, calls=%fused_computation.6.clone.1 | convolution fusion | flops 539492352 | bytes 3670017 | tf_op jit(solution)/shard_map/while/body/eval_jaxpr/kpqad,kqbd->kpab/dot_general | solution.py:32
  46.5 0.6 dynamic_slice.19
  47.7 1.3 %constant_dynamic-slice_fusion.2 = bf16[8,2,8,4096]{3,2,1,0:T(8,128)(2,1)S(1)} fusion(bf16[8,2,16,4096]{3,2,1,0:T(8,128)(2,1)} %get-tuple-element.138, s32[]{:T(128)S(6)} %select_n.131), kind=kLoop, calls=%fused_computation.16.clone.1 | loop fusion | bytes 2097156 | tf_op jit(solution)/shard_map/while/body/eval_jaxpr/dynamic_slice | solution.py:27
  49.1 0.6 gather_fusion
  49.7 0.1 copy.41
  49.8 2.3 %gather.20 = bf16[8,2,8,64,64]{4,3,2,0,1:T(8,128)(2,1)S(1)} reshape(bf16[8,2,8,4096]{3,2,0,1:T(8,128)(2,1)S(1)} %copy.41) | data formatting | bytes 2097152 | tf_op jit(solution)/shard_map/while/body/eval_jaxpr/jit(_take)/gather | solution.py:28
  52.1 0.0 copy-start.1
  52.1 1.6 %broadcast_select_fusion.4 = bf16[8,2,8,64,64]{4,3,2,0,1:T(8,128)(2,1)} fusion(bf16[8,2,8,64,64]{4,3,2,0,1:T(8,128)(2,1)S(1)} %gather.20, pred[8]{0:T(512)(128)(4,1)S(1)} %compare_and_fusion.3), kind=kLoop, calls=%fused_computation.7.clone.1 | loop fusion | flops 524288 | bytes 2097160 | tf_op jit(solution)/shard_map/while/body/eval_jaxpr/jit(_take)/select_n | solution.py:28
  53.7 8.1 %bitcast_add_fusion.3 = f32[8,8,64,64]{3,2,1,0:T(8,128)} fusion(f32[8,8,64,64]{3,2,1,0:T(8,128)} %get-tuple-element.125, bf16[8,2,8,64,64]{4,3,2,0,1:T(8,128)(2,1)} %broadcast_select_fusion.4, bf16[8,8,64,64]{3,2,1,0:T(8,128)(2,1)S(1)} %copy-done.1, pred[]{:T(512)S(6)} %compare.30), kind=kOutput, calls=%fused_computation.6.clone.1 | convolution fusion | flops 539492352 | bytes 3670017 | tf_op jit(solution)/shard_map/while/body/eval_jaxpr/kpqad,kqbd->kpab/dot_general | solution.py:32
  61.8 2.9 %reshape_reshape.7 = f32[4,2,8,4096]{3,2,1,0:T(8,128)} reshape(f32[8,8,64,64]{3,2,1,0:T(8,128)} %get-tuple-element.37) | data formatting | bytes 2097152 | tf_op jit(solution)/shard_map/reshape;reshape | solution.py:93
  64.7 3.6 %all-to-all-start.2 = ((f32[4,2,8,4096]{3,2,1,0:T(8,128)}), f32[4,2,8,4096]{3,2,1,0:T(8,128)S(1)}, u32[]{:S(2)}, u32[]{:S(2)}) async-start(f32[4,2,8,4096]{3,2,1,0:T(8,128)} %reshape_reshape.7), calls=%async_computation.2 | async-start | bytes 2097152 | tf_op jit(solution)/shard_map/all_to_all | solution.py:43
  68.3 0.0 all-reduce.3.cloned.1.call-start
  68.4 14.3 %all-to-all-done.2 = f32[4,2,8,4096]{3,2,1,0:T(8,128)S(1)} async-done(((f32[4,2,8,4096]{3,2,1,0:T(8,128)}), f32[4,2,8,4096]{3,2,1,0:T(8,128)S(1)}, u32[]{:S(2)}, u32[]{:S(2)}) %all-to-all-start.2) | async-done | bytes 1048608 | tf_op jit(solution)/shard_map/all_to_all | solution.py:43
  82.7 0.6 gather_fusion.1
  83.3 0.9 broadcast_select_fusion.1
  84.3 0.0 all-reduce.3.cloned.1.call-update
  84.3 0.6 dynamic-slice
  85.5 0.2 fusion.18
  85.7 28.0 %all-reduce.3.cloned.1.call-done = f32[4,8,4096]{2,1,0:T(8,128)} async-done(((f32[4,8,4096]{2,1,0:T(8,128)}), f32[4,8,4096]{2,1,0:T(8,128)}) %all-reduce.3.cloned.1.call-update) | async-done | bytes 524304
  113.8 1.9 %fusion.10 = bf16[4,4,4096]{2,1,0:T(4,128)(2,1)} fusion(bf16[4,8,4096]{2,1,0:T(8,128)(2,1)S(1)} %broadcast_select_fusion.2, f32[4,8,4096]{2,1,0:T(8,128)} %all-reduce.3.cloned.1.call-done, u32[]{:T(128)S(6)} %multiply.1, bf16[4,4,8]{2,0,1:T(4,128)(2,1)S(1)} %dynamic-slice_convert_fusion), kind=kOutput, calls=%fused_computation.19 | convolution fusion | flops 1179648 | bytes 655620 | tf_op jit(solution)/shard_map/kpq,kqx->kpx/dot_general | solution.py:78
  (19 shorter events, 0.2 us)
Async XLA Ops:
  6.5 79.0 %copy-start = (bf16[64,8,8]{0,2,1:T(8,128)(2,1)S(1)}, bf16[64,8,8]{0,2,1:T(8,128)(2,1)}, u32[]{:S(2)}) copy-start(bf16[64,8,8]{0,2,1:T(8,128)(2,1)} %param.12) | copy-start | bytes 24580
  9.2 8.1 %all-to-all-start = ((bf16[4,1,2]{2,1,0:T(2,128)(2,1)}), bf16[4,1,2]{2,1,0:T(2,128)(2,1)S(1)}, u32[]{:S(2)}, u32[]{:S(2)}) async-start(bf16[4,1,2]{2,1,0:T(2,128)(2,1)} %convert_element_type.67), calls=%async_computation | async-start | bytes 4096 | tf_op jit(solution)/shard_map/all_to_all | solution.py:87
  17.3 12.3 %all-to-all-start.1 = ((bf16[4,2,8,4096]{3,1,2,0:T(2,128)(2,1)}), bf16[4,2,8,4096]{3,1,2,0:T(2,128)(2,1)S(1)}, u32[]{:S(2)}, u32[]{:S(2)}) async-start(bf16[4,2,8,4096]{3,1,2,0:T(2,128)(2,1)} %copy.27), calls=%async_computation.1 | async-start | bytes 1048576 | tf_op jit(solution)/shard_map/all_to_all | solution.py:86
  37.5 1.6 %copy-start.1 = (bf16[8,8,64,64]{3,2,1,0:T(8,128)(2,1)S(1)}, bf16[8,8,64,64]{3,2,1,0:T(8,128)(2,1)}, u32[]{:S(2)}) copy-start(bf16[8,8,64,64]{3,2,1,0:T(8,128)(2,1)} %get-tuple-element.139) | copy-start | bytes 1572868 | tf_op jit(solution)/shard_map/while
  52.1 1.6 %copy-start.1 = (bf16[8,8,64,64]{3,2,1,0:T(8,128)(2,1)S(1)}, bf16[8,8,64,64]{3,2,1,0:T(8,128)(2,1)}, u32[]{:S(2)}) copy-start(bf16[8,8,64,64]{3,2,1,0:T(8,128)(2,1)} %get-tuple-element.139) | copy-start | bytes 1572868 | tf_op jit(solution)/shard_map/while
  64.7 19.6 %copy-start.2 = (u32[32]{0:T(128)S(1)}, u32[32]{0:T(128)}, u32[]{:S(2)}) copy-start(u32[32]{0:T(128)} %constant.90) | copy-start | bytes 388
  64.7 18.1 %all-to-all-start.2 = ((f32[4,2,8,4096]{3,2,1,0:T(8,128)}), f32[4,2,8,4096]{3,2,1,0:T(8,128)S(1)}, u32[]{:S(2)}, u32[]{:S(2)}) async-start(f32[4,2,8,4096]{3,2,1,0:T(8,128)} %reshape_reshape.7), calls=%async_computation.2 | async-start | bytes 2097152 | tf_op jit(solution)/shard_map/all_to_all | solution.py:43
  68.3 45.4 %all-reduce.3.cloned.1.call-start = ((), (), s32[]{:S(2)}) async-start(), calls=%async_computation.3 | async-start | bytes 1048576
Sparse Core Ops, SparseCore 0:
  84.4 29.3 all-reduce.2
where the time goes:
time: 123 us
  waiting for transfers between devices  51.1 us (42%)
  local copies, waits for them, and re-layouts  19.4 us (16%)
  matrix products  18 us (15%)
  between operations  14.1 us (11%)
  starting transfers between devices  11.4 us (9%)
  other arithmetic  7.13 us (6%)
  loops' own time  1.37 us (1%)
    unnamed x2, waiting for transfers between devices  28 us
    dot_general x2, matrix products, step(): jnp.einsum('kpqad,kqbd->kpab', middle, picked[:, 1], preferred_element_ty...  15.5 us
    all_to_all x1, waiting for transfers between devices, send_back(): lax.all_to_all(values, 'tile', split_axis=0, concat_axis=0, tiled=True)  14.3 us
    all_to_all x1, waiting for transfers between devices, local(): lax.all_to_all(packed, 'tile', split_axis=0, concat_axis=0, tiled=True)  8.7 us
    gather x6, local copies, waits for them, and re-layouts, step(): picked = jnp.take(portion, index, axis=0).reshape(count, 2, group, VB, VB)  5.99 us
    all_to_all x1, starting transfers between devices, local(): lax.all_to_all(labels, 'tile', split_axis=0, concat_axis=0, tiled=True)  4.24 us
    all_to_all x1, starting transfers between devices, send_back(): lax.all_to_all(values, 'tile', split_axis=0, concat_axis=0, tiled=True)  3.65 us
    all_to_all x1, starting transfers between devices, local(): lax.all_to_all(packed, 'tile', split_axis=0, concat_axis=0, tiled=True)  3.47 us
  transfers between devices with their start and end apart: 4, of which 3 were waited for; matrix products, arithmetic and copies ran while one was open for 4% of the time, Pallas kernels for 0%

commit v1 on v0

v1 whole, which is shorter than its diff:
```python
import functools

import jax
import jax.numpy as jnp
from jax import lax
from jax.experimental import pallas as pl
from jax.experimental.pallas import tpu as pltpu
from jax.sharding import PartitionSpec as P

VB = 64
CAP = 2
LANES = 128
HALF = VB // 2
QG = 4
MESH = pl.DeviceIdType.MESH


def low_half(rows):
    return lax.broadcasted_iota(jnp.int32, (rows, LANES), 1) < VB


def swap(value):
    return pltpu.roll(value, VB, 1)


def pair_rows(first, second):
    low = low_half(first.shape[0])
    even = jnp.where(low, first, swap(second))
    odd = jnp.where(low, swap(first), second)
    return even, odd


def spread_rows(value, wide):
    n = value.shape[0]
    for j in range(HALF):
        wide[pl.ds(j * n, n), :] = value[:, j * LANES:(j + 1) * LANES]


def kernel(
    peers, reps, tiles, depth, share, rows,
    blocks_ref, live_ref, owner_ref, amp_ref, coup_ref, fac_hbm,
    out_ref,
    fac, wide, cwide, ctile, packed, xs, xr, tag_send, tag_recv, tag_smem,
    left, right, weight, mid, result, kept, rs_send, rs_recv, back, ret, cyc,
    fac_sem, tag_local, tag_ssem, tag_rsem, x_ssem, x_rsem, rs_ssem, rs_rsem, b_ssem, b_rsem,
):
    groups = depth // QG
    chips = peers // 2
    slots = peers * CAP
    owned = fac_hbm.shape[0]
    me = lax.axis_index("tile")
    my_rep = lax.axis_index("rep")
    my_chip, my_core = me // 2, me % 2

    def to_peer(o):
        return (my_chip + o // 2) % chips * 2 + (my_core + o % 2) % 2

    def from_peer(o):
        return (my_chip + chips - o // 2) % chips * 2 + (my_core + o % 2) % 2

    def rep_peer(i):
        return (my_rep + i) % reps

    factors_copy = pltpu.make_async_copy(fac_hbm, fac, fac_sem)
    factors_copy.start()

    barrier = pltpu.get_barrier_semaphore()

    @pl.loop(1, peers)
    def _(o):
        pl.semaphore_signal(barrier, inc=1, device_id={"tile": to_peer(o)}, device_id_type=MESH)

    for i in range(1, reps):
        pl.semaphore_signal(barrier, inc=1, device_id={"rep": rep_peer(i)}, device_id_type=MESH)

    target, within, slot = [], [], []
    for k in range(tiles):
        place = owner_ref[blocks_ref[k, 1]]
        t = place // owned
        rank = 0
        for e in range(k):
            rank = rank + jnp.where(target[e] == t, 1, 0)
        m = (t // 2 + chips - my_chip) % chips
        c = (t % 2 + 2 - my_core) % 2
        target.append(t)
        within.append(place - t * owned)
        slot.append((m * 2 + c) * CAP + jnp.minimum(rank, CAP - 1))

    @pl.loop(0, tiles)
    def _(k):
        live = live_ref[k]
        row = lax.broadcasted_iota(jnp.int32, (rows, VB * VB), 0)
        masked = jnp.where(row < live, amp_ref[k].astype(jnp.float32), 0.0)
        spread_rows(masked, wide)
        for pair in range(rows // 2):
            first = wide[pl.ds(2 * pair, HALF, stride=rows), :]
            second = wide[pl.ds(2 * pair + 1, HALF, stride=rows), :]
            even, odd = pair_rows(first, second)
            ctile[pl.ds(pair * VB, HALF, stride=2), :] = even
            ctile[pl.ds(pair * VB + 1, HALF, stride=2), :] = odd
        packed[k] = ctile[...].astype(jnp.bfloat16)

    @pl.loop(0, peers)
    def _(o):
        tags = jnp.zeros((8, LANES), jnp.int32)
        row = lax.broadcasted_iota(jnp.int32, (8, LANES), 0)
        for j in range(CAP):
            s = o * CAP + j
            pick, tag = 0, 0
            for k in range(tiles):
                hit = slot[k] == s
                pick = jnp.where(hit, k, pick)
                tag = jnp.where(hit, within[k], tag)
            tags = jnp.where(row == j, tag, tags)
            xs[s] = packed[pick]
        tag_send[o] = tags

    pl.semaphore_wait(barrier, peers - 1 + reps - 1)

    def tag_copy(o):
        return pltpu.make_async_remote_copy(
            src_ref=tag_send.at[o], dst_ref=tag_recv.at[o], send_sem=tag_ssem.at[o], recv_sem=tag_rsem.at[o],
            device_id={"tile": to_peer(o)}, device_id_type=MESH)

    def x_copy(s):
        return pltpu.make_async_remote_copy(
            src_ref=xs.at[s], dst_ref=xr.at[s], send_sem=x_ssem.at[s], recv_sem=x_rsem.at[s],
            device_id={"tile": to_peer(s // CAP)}, device_id_type=MESH)

    def rs_copy(s, i):
        return pltpu.make_async_remote_copy(
            src_ref=rs_send.at[s, i - 1], dst_ref=rs_recv.at[s, i - 1],
            send_sem=rs_ssem.at[s, i - 1], recv_sem=rs_rsem.at[s, i - 1],
            device_id={"rep": rep_peer(i)}, device_id_type=MESH)

    def back_copy(s):
        return pltpu.make_async_remote_copy(
            src_ref=back.at[s], dst_ref=ret.at[s], send_sem=b_ssem.at[s], recv_sem=b_rsem.at[s],
            device_id={"tile": from_peer(s // CAP)}, device_id_type=MESH)

    def to_smem(o, source):
        return pltpu.make_async_copy(source.at[o], tag_smem.at[o], tag_local.at[o])

    @pl.loop(1, peers)
    def _(o):
        tag_copy(o).start()

    @pl.loop(CAP, slots)
    def _(s):
        x_copy(s).start()

    to_smem(0, tag_send).start()

    @pl.loop(0, tiles)
    def _(k):
        live = live_ref[k]
        row = lax.broadcasted_iota(jnp.int32, (rows, VB * VB), 0)
        masked = jnp.where(row < live, amp_ref[k].astype(jnp.float32), 0.0).astype(jnp.bfloat16)
        terms = jnp.dot(coup_ref[blocks_ref[k, 0]], masked, preferred_element_type=jnp.float32)
        for r in range(reps):
            cyc[k, r] = terms[r * share:(r + 1) * share]

    weight[...] = jnp.zeros_like(weight)
    to_smem(0, tag_send).wait()
    factors_copy.wait()

    low = low_half(VB)

    def compute(message, block):
        for pair in range(rows // 2):
            value = message[pl.ds(pair * VB, VB), :].astype(jnp.float32)
            turned = swap(value)
            for e, (a, b) in enumerate(((value, turned), (turned, value))):
                top = jnp.where(low, a, 0.0).astype(jnp.bfloat16)
                bottom = jnp.where(low, 0.0, b).astype(jnp.bfloat16)
                p = 2 * pair + e
                weight[p, 0:VB, 0:LANES] = top
                weight[p, VB:2 * VB, 0:LANES] = bottom
                weight[p, 2 * VB:3 * VB, LANES:] = top
                weight[p, 3 * VB:, LANES:] = bottom
        spread_rows(fac[block, 0].astype(jnp.float32), cwide)
        for pair in range(depth // 2):
            first = cwide[pl.ds(2 * pair, HALF, stride=depth), :]
            second = cwide[pl.ds(2 * pair + 1, HALF, stride=depth), :]
            even, odd = pair_rows(first, second)
            g, h = pair // 2, pair % 2
            left[pl.ds(g * VB, HALF), h * LANES:(h + 1) * LANES] = even.astype(jnp.bfloat16)
            left[pl.ds(g * VB + HALF, HALF), h * LANES:(h + 1) * LANES] = odd.astype(jnp.bfloat16)
        spread_rows(fac[block, 1].astype(jnp.float32), cwide)
        for pair in range(depth // 2):
            first = cwide[pl.ds(2 * pair, HALF, stride=depth), :]
            second = cwide[pl.ds(2 * pair + 1, HALF, stride=depth), :]
            even, odd = pair_rows(first, second)
            ctile[pl.ds(0, HALF, stride=2), :] = even
            ctile[pl.ds(1, HALF, stride=2), :] = odd
            value = ctile[pl.ds(0, VB), :].astype(jnp.bfloat16)
            g, h = pair // 2, pair % 2
            right[g, 0:VB, h * LANES:(h + 1) * LANES] = value
            right[g, VB:, h * LANES:(h + 1) * LANES] = value
        for p in range(rows):
            part = jnp.dot(left[...], weight[p], preferred_element_type=jnp.float32).astype(jnp.bfloat16)
            for g in range(groups):
                mid[g, pl.ds(p * VB, VB), :] = part[g * VB:(g + 1) * VB]
        total = jnp.zeros((rows * VB, LANES), jnp.float32)
        for g in range(groups):
            total = total + lax.dot_general(
                mid[g], right[g], (((1,), (1,)), ((), ())), preferred_element_type=jnp.float32)
        total = total.reshape(rows, 2, HALF, LANES)
        result[...] = jnp.where(low_half(HALF)[None], total[:, 0], total[:, 1])

    def after(s):
        kept[s] = result[pl.ds(my_rep * share, share)].reshape(share * HALF, LANES)
        for i in range(1, reps):
            part = result[pl.ds(rep_peer(i) * share, share)].reshape(share * HALF, LANES)
            rs_send[s, i - 1] = part.astype(jnp.bfloat16)
            rs_copy(s, i).start()

    def summed(s):
        total = kept[s]
        for i in range(1, reps):
            rs_copy(s, i).wait_recv()
            total = total + rs_recv[s, i - 1].astype(jnp.float32)
        return total.astype(jnp.bfloat16)

    def finish(s):
        back[s] = summed(s)
        back_copy(s).start()

    for j in range(CAP):
        xr[j] = xs[j]

    @pl.loop(0, slots)
    def _(s):
        o = s // CAP

        @pl.when(s >= CAP)
        def _():
            x_copy(s).wait_recv()

            @pl.when(s % CAP == 0)
            def _():
                tag_copy(o).wait_recv()
                fetch = to_smem(o, tag_recv)
                fetch.start()
                fetch.wait()

        compute(xr.at[s], tag_smem[o, s % CAP, 0])
        after(s)

        @pl.when(s > CAP)
        def _():
            finish(s - 1)

    for j in range(CAP):
        ret[j] = summed(j)
    finish(slots - 1)

    @pl.loop(CAP, slots)
    def _(s):
        back_copy(s).wait_recv()

    for k in range(tiles):
        wide[pl.ds(0, share * HALF), :] = ret[slot[k]].astype(jnp.float32)
        mine = cyc[k, my_rep]
        for j in range(HALF):
            part = wide[pl.ds(j, share, stride=HALF), :] + mine[:, j * LANES:(j + 1) * LANES]
            out_ref[k, :, j * LANES:(j + 1) * LANES] = part.astype(out_ref.dtype)

    @pl.loop(1, peers)
    def _(o):
        tag_copy(o).wait_send()

    @pl.loop(CAP, slots)
    def _(s):
        x_copy(s).wait_send()
        back_copy(s).wait_send()

    @pl.loop(0, slots)
    def _(s):
        for i in range(1, reps):
            rs_copy(s, i).wait_send()


def solution(mesh):
    peers, reps = mesh.shape["tile"], mesh.shape["rep"]

    def local(amplitudes, tile_blocks, live_rows, ladder_factors, cycle_coupling, block_owner):
        tiles, rows, cells = amplitudes.shape
        owned, _, depth, _ = ladder_factors.shape
        share = rows // reps
        slots = peers * CAP
        groups = depth // QG
        bf16, f32, dma = jnp.bfloat16, jnp.float32, pltpu.SemaphoreType.DMA
        smem, vmem = pltpu.SMEM, pltpu.VMEM
        return pl.pallas_call(
            functools.partial(kernel, peers, reps, tiles, depth, share, rows),
            out_shape=jax.ShapeDtypeStruct((tiles, share, cells), bf16),
            in_specs=[pl.BlockSpec(memory_space=smem)] * 3
            + [pl.BlockSpec(memory_space=vmem)] * 2
            + [pl.BlockSpec(memory_space=pl.ANY)],
            out_specs=pl.BlockSpec(memory_space=vmem),
            scratch_shapes=[
                vmem((owned, 2, depth, cells), bf16),
                vmem((rows * HALF, LANES), f32),
                vmem((depth * HALF, LANES), f32),
                vmem((rows // 2 * VB, LANES), f32),
                vmem((tiles, rows // 2 * VB, LANES), bf16),
                vmem((slots, rows // 2 * VB, LANES), bf16),
                vmem((slots, rows // 2 * VB, LANES), bf16),
                vmem((peers, 8, LANES), jnp.int32),
                vmem((peers, 8, LANES), jnp.int32),
                smem((peers, 8, LANES), jnp.int32),
                vmem((groups * VB, QG * VB), bf16),
                vmem((groups, LANES, QG * VB), bf16),
                vmem((rows, QG * VB, QG * VB), bf16),
                vmem((groups, rows * VB, QG * VB), bf16),
                vmem((rows, HALF, LANES), f32),
                vmem((slots, share * HALF, LANES), f32),
                vmem((slots, reps - 1, share * HALF, LANES), bf16),
                vmem((slots, reps - 1, share * HALF, LANES), bf16),
                vmem((slots, share * HALF, LANES), bf16),
                vmem((slots, share * HALF, LANES), bf16),
                vmem((tiles, reps, share, cells), f32),
                dma,
                dma((peers,)),
                dma((peers,)),
                dma((peers,)),
                dma((slots,)),
                dma((slots,)),
                dma((slots, reps - 1)),
                dma((slots, reps - 1)),
                dma((slots,)),
                dma((slots,)),
            ],
            compiler_params=pltpu.CompilerParams(
                collective_id=0, has_side_effects=True, vmem_limit_bytes=48 * 2**20
            ),
            name="ladder",
        )(tile_blocks, live_rows, block_owner, amplitudes, cycle_coupling, ladder_factors)

    placed = (
        P(("grp", "tile"), None, None),
        P(("grp", "tile"), None),
        P(("grp", "tile")),
        P("tile", None, "rep", None),
        P(),
        P(),
    )
    return jax.shard_map(
        local,
        mesh=mesh,
        in_specs=placed,
        out_specs=P(("grp", "tile"), "rep", None),
        check_vma=False,
    )
```

time: 123 us -> 30.9 us (0.25)
  the two profiles are of different devices: /device:TPU:0 before, /device:TPU:1 now
where the time goes in v1:
time: 30.9 us; the launch traced here: 30.6 us
  Pallas kernels  24.4 us (79%)
  local copies, waits for them, and re-layouts  6.11 us (20%)
    pallas_call x1, Pallas kernels, local(): pl.pallas_call(functools.partial(kernel, peers, reps, tiles, depth, share...  24.4 us
    unnamed x11, local copies, waits for them, and re-layouts  6.11 us

profile of v1, /device:TPU:1, one launch (start us, length us, event | category | flops | bytes accessed | tf_op | source)
XLA Modules:
  0.0 30.6 jit_solution(13390268885551285341)
XLA Ops:
  0.0 0.8 %copy.7.blocks_ref = s32[4,2]{1,0:T(4,128)S(1)} copy(s32[4,2]{0,1:T(2,128)} %param.7) | data formatting | bytes 64 | tf_op args[1]
  0.8 0.8 %copy.8.coup_ref = bf16[64,8,8]{2,1,0:T(8,128)(2,1)S(1)} copy(bf16[64,8,8]{0,2,1:T(8,128)(2,1)} %param.10) | data formatting | bytes 16384 | tf_op args[4]
  1.6 0.0 copy-start
  1.6 1.6 %copy-done = bf16[8,2,16,4096]{3,2,1,0:T(8,128)(2,1)S(1)} copy-done((bf16[8,2,16,4096]{3,2,1,0:T(8,128)(2,1)S(1)}, bf16[8,2,16,4096]{3,2,1,0:T(8,128)(2,1)}, u32[]{:S(2)}) %copy-start) | copy-done | bytes 2097176
  3.2 0.0 copy-start.1
  3.2 0.9 %copy-done.1 = bf16[4,8,4096]{2,1,0:T(8,128)(2,1)S(1)} copy-done((bf16[4,8,4096]{2,1,0:T(8,128)(2,1)S(1)}, bf16[4,8,4096]{2,1,0:T(8,128)(2,1)}, u32[]{:S(2)}) %copy-start.1) | copy-done | bytes 262168
  4.2 0.0 copy-start.2
  4.2 0.7 %copy-done.2 = s32[4]{0:T(128)S(1)} copy-done((s32[4]{0:T(128)S(1)}, s32[4]{0:T(128)}, u32[]{:S(2)}) %copy-start.2) | copy-done | bytes 40
  4.8 0.0 copy-start.3
  4.8 0.7 %copy-done.3 = s32[32]{0:T(128)S(1)} copy-done((s32[32]{0:T(128)S(1)}, s32[32]{0:T(128)}, u32[]{:S(2)}) %copy-start.3) | copy-done | bytes 152
  5.5 24.4 %ladder.1 = bf16[4,4,4096]{2,1,0:T(4,128)(2,1)S(1)} custom-call(s32[4,2]{1,0:T(4,128)S(1)} %copy.7.blocks_ref, s32[4]{0:T(128)S(1)} %copy-done.2, s32[32]{0:T(128)S(1)} %copy-done.3, bf16[4,8,4096]{2,1,0:T(8,128)(2,1)S(1)} %copy-done.1, bf16[64,8,8]{2,1,0:T(8,128)(2,1)S(1)} %copy.8.coup_ref, bf16[8,2,16,4096]{3,2,1,0:T(8,128)(2,1)S(1)} %copy-done), custom_call_target="tpu_custom_call" | custom-call | tf_op jit(solution)/shard_map/ladder/pallas_call | solution.py:295
  29.9 0.7 %copy.10 = bf16[4,4,4096]{2,1,0:T(4,128)(2,1)} copy(bf16[4,4,4096]{2,1,0:T(4,128)(2,1)S(1)} %ladder.1) | data formatting | bytes 262144
Async XLA Ops:
  1.6 1.6 %copy-start = (bf16[8,2,16,4096]{3,2,1,0:T(8,128)(2,1)S(1)}, bf16[8,2,16,4096]{3,2,1,0:T(8,128)(2,1)}, u32[]{:S(2)}) copy-start(bf16[8,2,16,4096]{3,2,1,0:T(8,128)(2,1)} %fac_hbm.1) | copy-start | bytes 6291460
  3.2 0.9 %copy-start.1 = (bf16[4,8,4096]{2,1,0:T(8,128)(2,1)S(1)}, bf16[4,8,4096]{2,1,0:T(8,128)(2,1)}, u32[]{:S(2)}) copy-start(bf16[4,8,4096]{2,1,0:T(8,128)(2,1)} %amp_ref.1) | copy-start | bytes 786436
  4.2 0.7 %copy-start.2 = (s32[4]{0:T(128)S(1)}, s32[4]{0:T(128)}, u32[]{:S(2)}) copy-start(s32[4]{0:T(128)} %live_ref.1) | copy-start | bytes 52
  4.8 0.7 %copy-start.3 = (s32[32]{0:T(128)S(1)}, s32[32]{0:T(128)}, u32[]{:S(2)}) copy-start(s32[32]{0:T(128)} %owner_ref.1) | copy-start | bytes 388

commit v2 on v1

v2 whole, which is shorter than its diff:
```python
import functools

import jax
import jax.numpy as jnp
from jax import lax
from jax.experimental import pallas as pl
from jax.experimental.pallas import tpu as pltpu
from jax.sharding import PartitionSpec as P

VB = 64
CAP = 2
LANES = 128
HALF = VB // 2
QG = 4
MESH = pl.DeviceIdType.MESH


def low_half(rows):
    return lax.broadcasted_iota(jnp.int32, (rows, LANES), 1) < VB


def swap(value):
    return pltpu.roll(value, VB, 1)


def pair_rows(first, second):
    low = low_half(first.shape[0])
    even = jnp.where(low, first, swap(second))
    odd = jnp.where(low, swap(first), second)
    return even, odd


def spread_rows(value, wide):
    n = value.shape[0]
    for j in range(HALF):
        wide[pl.ds(j * n, n), :] = value[:, j * LANES:(j + 1) * LANES]


def kernel(
    peers, reps, tiles, depth, share, rows,
    blocks_hbm, live_hbm, owner_hbm, amp_hbm, coup_hbm, fac_hbm,
    out_ref,
    blocks_ref, live_ref, owner_ref, amp_ref, coup_ref, fac, wide, cwide, ctile, packed, xs, xr,
    tag_send, tag_recv, tag_smem, left, right, weight, mid, kept, rs_send, rs_recv, back, ret, cyc,
    in_sem, tag_local, tag_ssem, tag_rsem, x_ssem, x_rsem, rs_ssem, rs_rsem, b_ssem, b_rsem,
):
    groups = depth // QG
    chips = peers // 2
    slots = peers * CAP
    steps = slots // 2
    owned = fac_hbm.shape[0]
    me = lax.axis_index("tile")
    my_rep = lax.axis_index("rep")
    my_chip, my_core = me // 2, me % 2

    def to_peer(o):
        return (my_chip + o // 2) % chips * 2 + (my_core + o % 2) % 2

    def from_peer(o):
        return (my_chip + chips - o // 2) % chips * 2 + (my_core + o % 2) % 2

    def rep_peer(i):
        return (my_rep + i) % reps

    loads = [
        pltpu.make_async_copy(source, target, in_sem.at[n])
        for n, (source, target) in enumerate((
            (amp_hbm, amp_ref), (blocks_hbm, blocks_ref), (live_hbm, live_ref),
            (owner_hbm, owner_ref), (coup_hbm, coup_ref), (fac_hbm, fac)))
    ]
    for load in loads:
        load.start()

    barrier = pltpu.get_barrier_semaphore()

    @pl.loop(1, peers)
    def _(o):
        pl.semaphore_signal(barrier, inc=1, device_id={"tile": to_peer(o)}, device_id_type=MESH)

    for i in range(1, reps):
        pl.semaphore_signal(barrier, inc=1, device_id={"rep": rep_peer(i)}, device_id_type=MESH)

    for load in loads[1:4]:
        load.wait()

    target, within, slot = [], [], []
    for k in range(tiles):
        place = owner_ref[blocks_ref[1, k]]
        t = place // owned
        rank = 0
        for e in range(k):
            rank = rank + jnp.where(target[e] == t, 1, 0)
        m = (t // 2 + chips - my_chip) % chips
        c = (t % 2 + 2 - my_core) % 2
        target.append(t)
        within.append(place - t * owned)
        slot.append((m * 2 + c) * CAP + jnp.minimum(rank, CAP - 1))

    def in_slot(s):
        pick, tag = 0, 0
        for k in range(tiles):
            hit = slot[k] == s
            pick = jnp.where(hit, k, pick)
            tag = jnp.where(hit, within[k], tag)
        return pick, tag

    loads[0].wait()

    @pl.loop(0, tiles)
    def _(k):
        live = live_ref[k]
        row = lax.broadcasted_iota(jnp.int32, (rows, VB * VB), 0)
        masked = jnp.where(row < live, amp_ref[k].astype(jnp.float32), 0.0)
        spread_rows(masked, wide)
        for pair in range(rows // 2):
            first = wide[pl.ds(2 * pair, HALF, stride=rows), :]
            second = wide[pl.ds(2 * pair + 1, HALF, stride=rows), :]
            even, odd = pair_rows(first, second)
            ctile[pl.ds(pair * VB, HALF, stride=2), :] = even
            ctile[pl.ds(pair * VB + 1, HALF, stride=2), :] = odd
        packed[k] = ctile[...].astype(jnp.bfloat16)

    own_tags = []
    for j in range(CAP):
        pick, tag = in_slot(j)
        xr[j] = packed[pick]
        own_tags.append(tag)

    @pl.loop(1, peers)
    def _(o):
        tags = jnp.zeros((8, LANES), jnp.int32)
        row = lax.broadcasted_iota(jnp.int32, (8, LANES), 0)
        for j in range(CAP):
            pick, tag = in_slot(o * CAP + j)
            tags = jnp.where(row == j, tag, tags)
            xs[o * CAP + j] = packed[pick]
        tag_send[o] = tags

    pl.semaphore_wait(barrier, peers - 1 + reps - 1)

    def tag_copy(o):
        return pltpu.make_async_remote_copy(
            src_ref=tag_send.at[o], dst_ref=tag_recv.at[o], send_sem=tag_ssem.at[o], recv_sem=tag_rsem.at[o],
            device_id={"tile": to_peer(o)}, device_id_type=MESH)

    def x_copy(s):
        return pltpu.make_async_remote_copy(
            src_ref=xs.at[s], dst_ref=xr.at[s], send_sem=x_ssem.at[s], recv_sem=x_rsem.at[s],
            device_id={"tile": to_peer(s // CAP)}, device_id_type=MESH)

    def rs_copy(s, i):
        return pltpu.make_async_remote_copy(
            src_ref=rs_send.at[s, i - 1], dst_ref=rs_recv.at[s, i - 1],
            send_sem=rs_ssem.at[s, i - 1], recv_sem=rs_rsem.at[s, i - 1],
            device_id={"rep": rep_peer(i)}, device_id_type=MESH)

    def back_copy(s):
        return pltpu.make_async_remote_copy(
            src_ref=back.at[s], dst_ref=ret.at[s], send_sem=b_ssem.at[s], recv_sem=b_rsem.at[s],
            device_id={"tile": from_peer(s // CAP)}, device_id_type=MESH)

    def to_smem(o):
        return pltpu.make_async_copy(tag_recv.at[o], tag_smem.at[o], tag_local.at[o])

    @pl.loop(1, peers)
    def _(o):
        tag_copy(o).start()

    @pl.loop(CAP, slots)
    def _(s):
        x_copy(s).start()

    low = low_half(VB)

    def prepare(b, block):
        spread_rows(fac[block, 0].astype(jnp.float32), cwide.at[2 * b])
        spread_rows(fac[block, 1].astype(jnp.float32), cwide.at[2 * b + 1])
        for pair in range(depth // 2):
            first = cwide[2 * b, pl.ds(2 * pair, HALF, stride=depth), :]
            second = cwide[2 * b, pl.ds(2 * pair + 1, HALF, stride=depth), :]
            even, odd = pair_rows(first, second)
            g, h = pair // 2, pair % 2
            left[b, pl.ds(g * VB, HALF), h * LANES:(h + 1) * LANES] = even.astype(jnp.bfloat16)
            left[b, pl.ds(g * VB + HALF, HALF), h * LANES:(h + 1) * LANES] = odd.astype(jnp.bfloat16)
        for pair in range(depth // 2):
            first = cwide[2 * b + 1, pl.ds(2 * pair, HALF, stride=depth), :]
            second = cwide[2 * b + 1, pl.ds(2 * pair + 1, HALF, stride=depth), :]
            even, odd = pair_rows(first, second)
            ctile[pl.ds(pair % 2 * VB, HALF, stride=2), :] = even
            ctile[pl.ds(pair % 2 * VB + 1, HALF, stride=2), :] = odd
            value = ctile[pl.ds(pair % 2 * VB, VB), :].astype(jnp.bfloat16)
            right[b, 0:VB, pair * LANES:(pair + 1) * LANES] = value
            right[b, VB:, pair * LANES:(pair + 1) * LANES] = value

    def compute(b, s):
        message = xr.at[s]
        for pair in range(rows // 2):
            value = message[pl.ds(pair * VB, VB), :].astype(jnp.float32)
            turned = swap(value)
            for e, (one, two) in enumerate(((value, turned), (turned, value))):
                top = jnp.where(low, one, 0.0).astype(jnp.bfloat16)
                bottom = jnp.where(low, 0.0, two).astype(jnp.bfloat16)
                p = 2 * pair + e
                weight[b, p, 0:VB, 0:LANES] = top
                weight[b, p, VB:2 * VB, 0:LANES] = bottom
                weight[b, p, 2 * VB:3 * VB, LANES:] = top
                weight[b, p, 3 * VB:, LANES:] = bottom
        for p in range(rows):
            part = jnp.dot(left[b], weight[b, p], preferred_element_type=jnp.float32).astype(jnp.bfloat16)
            for g in range(groups):
                mid[b, pl.ds(p * VB, VB), g * QG * VB:(g + 1) * QG * VB] = part[g * VB:(g + 1) * VB]
        total = lax.dot_general(
            mid[b], right[b], (((1,), (1,)), ((), ())), preferred_element_type=jnp.float32)
        total = total.reshape(rows, 2, HALF, LANES)
        total = jnp.where(low_half(HALF)[None], total[:, 0], total[:, 1])
        for r in range(reps):
            kept[s, r] = total[r * share:(r + 1) * share].reshape(share * HALF, LANES)

    def exchange(s):
        for i in range(1, reps):
            rs_send[s, i - 1] = kept[s, rep_peer(i)].astype(jnp.bfloat16)
            rs_copy(s, i).start()

    def summed(s):
        total = kept[s, my_rep]
        for i in range(1, reps):
            rs_copy(s, i).wait_recv()
            total = total + rs_recv[s, i - 1].astype(jnp.float32)
        return total.astype(jnp.bfloat16)

    def finish(s):
        back[s] = summed(s)
        back_copy(s).start()

    loads[4].wait()

    @pl.loop(0, tiles)
    def _(k):
        live = live_ref[k]
        row = lax.broadcasted_iota(jnp.int32, (rows, VB * VB), 0)
        masked = jnp.where(row < live, amp_ref[k].astype(jnp.float32), 0.0).astype(jnp.bfloat16)
        coup = coup_ref[...].astype(jnp.float32)
        chosen = lax.broadcasted_iota(jnp.int32, coup.shape, 2) == blocks_ref[0, k]
        coup = jnp.sum(jnp.where(chosen, coup, 0.0), axis=2).astype(jnp.bfloat16)
        terms = jnp.dot(coup, masked, preferred_element_type=jnp.float32)
        for r in range(reps):
            cyc[k, r] = terms[r * share:(r + 1) * share]

    weight[...] = jnp.zeros_like(weight)
    loads[5].wait()
    prepare(0, own_tags[0])

    @pl.loop(1, peers)
    def _(o):
        tag_copy(o).wait_recv()
        to_smem(o).start()

    @pl.loop(1, peers)
    def _(o):
        to_smem(o).wait()

    @pl.loop(0, steps)
    def _(n):
        s0 = jnp.where(n == 0, 0, 2 * n + 1)
        s1 = jnp.where(n == steps - 1, 1, 2 * n + 2)
        s2 = jnp.where(n == steps - 1, CAP, 2 * n + 3)
        tag1 = jnp.where(n == steps - 1, own_tags[1], tag_smem[jnp.maximum(s1 // CAP, 1), s1 % CAP, 0])
        tag2 = tag_smem[s2 // CAP, s2 % CAP, 0]

        @pl.when(n > 0)
        def _():
            x_copy(s0).wait_recv()

        compute(0, s0)
        prepare(1, tag1)
        exchange(s0)

        @pl.when(n > 0)
        def _():
            finish(2 * n)

        @pl.when(n < steps - 1)
        def _():
            x_copy(s1).wait_recv()

        compute(1, s1)
        prepare(0, tag2)
        exchange(s1)

        @pl.when(n > 0)
        def _():
            finish(s0)

    for j in range(CAP):
        ret[j] = summed(j)

    @pl.loop(CAP, slots)
    def _(s):
        back_copy(s).wait_recv()

    for k in range(tiles):
        wide[pl.ds(0, share * HALF), :] = ret[slot[k]].astype(jnp.float32)
        mine = cyc[k, my_rep]
        for j in range(HALF):
            part = wide[pl.ds(j, share, stride=HALF), :] + mine[:, j * LANES:(j + 1) * LANES]
            out_ref[k, :, j * LANES:(j + 1) * LANES] = part.astype(out_ref.dtype)

    @pl.loop(1, peers)
    def _(o):
        tag_copy(o).wait_send()

    @pl.loop(CAP, slots)
    def _(s):
        x_copy(s).wait_send()
        back_copy(s).wait_send()

    @pl.loop(0, slots)
    def _(s):
        for i in range(1, reps):
            rs_copy(s, i).wait_send()


def solution(mesh):
    peers, reps = mesh.shape["tile"], mesh.shape["rep"]

    def local(amplitudes, tile_blocks, live_rows, ladder_factors, cycle_coupling, block_owner):
        tiles, rows, cells = amplitudes.shape
        owned, _, depth, _ = ladder_factors.shape
        share = rows // reps
        slots = peers * CAP
        groups = depth // QG
        bf16, f32, dma = jnp.bfloat16, jnp.float32, pltpu.SemaphoreType.DMA
        smem, vmem = pltpu.SMEM, pltpu.VMEM
        return pl.pallas_call(
            functools.partial(kernel, peers, reps, tiles, depth, share, rows),
            out_shape=jax.ShapeDtypeStruct((tiles, share, cells), bf16),
            in_specs=[pl.BlockSpec(memory_space=pl.ANY)] * 6,
            out_specs=pl.BlockSpec(memory_space=vmem),
            scratch_shapes=[
                smem(tile_blocks.shape[::-1], jnp.int32),
                smem(live_rows.shape, jnp.int32),
                smem(block_owner.shape, jnp.int32),
                vmem(amplitudes.shape, bf16),
                vmem((rows, rows, cycle_coupling.shape[0]), bf16),
                vmem(ladder_factors.shape, bf16),
                vmem((rows * HALF, LANES), f32),
                vmem((4, depth * HALF, LANES), f32),
                vmem((rows // 2 * VB, LANES), f32),
                vmem((tiles, rows // 2 * VB, LANES), bf16),
                vmem((slots, rows // 2 * VB, LANES), bf16),
                vmem((slots, rows // 2 * VB, LANES), bf16),
                vmem((peers, 8, LANES), jnp.int32),
                vmem((peers, 8, LANES), jnp.int32),
                smem((peers, 8, LANES), jnp.int32),
                vmem((2, groups * VB, QG * VB), bf16),
                vmem((2, LANES, depth * VB), bf16),
                vmem((2, rows, QG * VB, QG * VB), bf16),
                vmem((2, rows * VB, depth * VB), bf16),
                vmem((slots, reps, share * HALF, LANES), f32),
                vmem((slots, reps - 1, share * HALF, LANES), bf16),
                vmem((slots, reps - 1, share * HALF, LANES), bf16),
                vmem((slots, share * HALF, LANES), bf16),
                vmem((slots, share * HALF, LANES), bf16),
                vmem((tiles, reps, share, cells), f32),
                dma((6,)),
                dma((peers,)),
                dma((peers,)),
                dma((peers,)),
                dma((slots,)),
                dma((slots,)),
                dma((slots, reps - 1)),
                dma((slots, reps - 1)),
                dma((slots,)),
                dma((slots,)),
            ],
            compiler_params=pltpu.CompilerParams(
                collective_id=0, has_side_effects=True, vmem_limit_bytes=62 * 2**20
            ),
            name="ladder",
        )(
            tile_blocks.T, live_rows, block_owner, amplitudes,
            jnp.transpose(cycle_coupling, (1, 2, 0)), ladder_factors)

    placed = (
        P(("grp", "tile"), None, None),
        P(("grp", "tile"), None),
        P(("grp", "tile")),
        P("tile", None, "rep", None),
        P(),
        P(),
    )
    return jax.shard_map(
        local,
        mesh=mesh,
        in_specs=placed,
        out_specs=P(("grp", "tile"), "rep", None),
        check_vma=False,
    )
```

time: 30.9 us -> 28.2 us (0.913)
  the two profiles are of different devices: /device:TPU:1 before, /device:TPU:0 now
where the time goes in v2:
time: 28.2 us; the launch traced here: 28 us
  Pallas kernels  26.4 us (94%)
  local copies, waits for them, and re-layouts  1.61 us (6%)
    pallas_call x1, Pallas kernels, local(): pl.pallas_call(functools.partial(kernel, peers, reps, tiles, depth, share...  26.4 us
    unnamed x1, local copies, waits for them, and re-layouts  1.61 us

profile of v2, /device:TPU:0, one launch (start us, length us, event | category | flops | bytes accessed | tf_op | source)
XLA Modules:
  0.0 28.0 jit_solution(11766795291637270936)
XLA Ops:
  0.0 26.4 %ladder.1 = bf16[4,4,4096]{2,1,0:T(4,128)(2,1)} custom-call(s32[2,4]{1,0:T(2,128)} %bitcast.3, s32[4]{0:T(128)} %live_hbm.1, s32[32]{0:T(128)} %owner_hbm.1, bf16[4,8,4096]{2,1,0:T(8,128)(2,1)} %amp_hbm.1, bf16[8,8,64]{2,1,0:T(8,128)(2,1)} %bitcast.2, bf16[8,2,16,4096]{3,2,1,0:T(8,128)(2,1)} %fac_hbm.1), custom_call_target="tpu_custom_call" | custom-call | tf_op jit(solution)/shard_map/ladder/pallas_call | solution.py:334
  26.4 1.6 %copy.8 = bf16[4,4,4096]{2,1,0:T(4,128)(2,1)} copy(bf16[4,4,4096]{2,1,0:T(4,128)(2,1)} %ladder.1) | data formatting | bytes 262144

commit v3 on v2

--- a/solution.py
+++ b/solution.py
@@ -11,7 +11,6 @@
 CAP = 2
 LANES = 128
 HALF = VB // 2
-QG = 4
 MESH = pl.DeviceIdType.MESH
 
 
@@ -41,10 +40,9 @@
     blocks_hbm, live_hbm, owner_hbm, amp_hbm, coup_hbm, fac_hbm,
     out_ref,
     blocks_ref, live_ref, owner_ref, amp_ref, coup_ref, fac, wide, cwide, ctile, packed, xs, xr,
-    tag_send, tag_recv, tag_smem, left, right, weight, mid, kept, rs_send, rs_recv, back, ret, cyc,
+    tag_send, tag_recv, tag_smem, left, right, mid, kept, rs_send, rs_recv, back, ret, cyc,
     in_sem, tag_local, tag_ssem, tag_rsem, x_ssem, x_rsem, rs_ssem, rs_rsem, b_ssem, b_rsem,
 ):
-    groups = depth // QG
     chips = peers // 2
     slots = peers * CAP
     steps = slots // 2
@@ -173,42 +171,43 @@
     low = low_half(VB)
 
     def prepare(b, block):
-        spread_rows(fac[block, 0].astype(jnp.float32), cwide.at[2 * b])
-        spread_rows(fac[block, 1].astype(jnp.float32), cwide.at[2 * b + 1])
-        for pair in range(depth // 2):
+        def spread():
+            spread_rows(fac[block, 0].astype(jnp.float32), cwide.at[2 * b])
+            spread_rows(fac[block, 1].astype(jnp.float32), cwide.at[2 * b + 1])
+
+        def both(pair):
             first = cwide[2 * b, pl.ds(2 * pair, HALF, stride=depth), :]
             second = cwide[2 * b, pl.ds(2 * pair + 1, HALF, stride=depth), :]
             even, odd = pair_rows(first, second)
-            g, h = pair // 2, pair % 2
-            left[b, pl.ds(g * VB, HALF), h * LANES:(h + 1) * LANES] = even.astype(jnp.bfloat16)
-            left[b, pl.ds(g * VB + HALF, HALF), h * LANES:(h + 1) * LANES] = odd.astype(jnp.bfloat16)
-        for pair in range(depth // 2):
+            left[b, pl.ds(pair * VB, HALF), :] = even.astype(jnp.bfloat16)
+            left[b, pl.ds(pair * VB + HALF, HALF), :] = odd.astype(jnp.bfloat16)
             first = cwide[2 * b + 1, pl.ds(2 * pair, HALF, stride=depth), :]
             second = cwide[2 * b + 1, pl.ds(2 * pair + 1, HALF, stride=depth), :]
             even, odd = pair_rows(first, second)
-            ctile[pl.ds(pair % 2 * VB, HALF, stride=2), :] = even
-            ctile[pl.ds(pair % 2 * VB + 1, HALF, stride=2), :] = odd
-            value = ctile[pl.ds(pair % 2 * VB, VB), :].astype(jnp.bfloat16)
+            ctile[pl.ds(pair % 4 * VB, HALF, stride=2), :] = even
+            ctile[pl.ds(pair % 4 * VB + 1, HALF, stride=2), :] = odd
+            value = ctile[pl.ds(pair % 4 * VB, VB), :].astype(jnp.bfloat16)
             right[b, 0:VB, pair * LANES:(pair + 1) * LANES] = value
             right[b, VB:, pair * LANES:(pair + 1) * LANES] = value
 
-    def compute(b, s):
+        return [spread] + [functools.partial(both, pair) for pair in range(depth // 2)]
+
+    def compute(b, s, beside):
         message = xr.at[s]
+        each = -(-len(beside) // (rows // 2))
         for pair in range(rows // 2):
             value = message[pl.ds(pair * VB, VB), :].astype(jnp.float32)
             turned = swap(value)
-            for e, (one, two) in enumerate(((value, turned), (turned, value))):
-                top = jnp.where(low, one, 0.0).astype(jnp.bfloat16)
-                bottom = jnp.where(low, 0.0, two).astype(jnp.bfloat16)
-                p = 2 * pair + e
-                weight[b, p, 0:VB, 0:LANES] = top
-                weight[b, p, VB:2 * VB, 0:LANES] = bottom
-                weight[b, p, 2 * VB:3 * VB, LANES:] = top
-                weight[b, p, 3 * VB:, LANES:] = bottom
-        for p in range(rows):
-            part = jnp.dot(left[b], weight[b, p], preferred_element_type=jnp.float32).astype(jnp.bfloat16)
-            for g in range(groups):
-                mid[b, pl.ds(p * VB, VB), g * QG * VB:(g + 1) * QG * VB] = part[g * VB:(g + 1) * VB]
+            top = jnp.concatenate([jnp.where(low, value, 0.0), jnp.where(low, turned, 0.0)], axis=1)
+            bottom = jnp.concatenate([jnp.where(low, 0.0, turned), jnp.where(low, 0.0, value)], axis=1)
+            weight = jnp.concatenate([top.astype(jnp.bfloat16), bottom.astype(jnp.bfloat16)], axis=0)
+            part = jnp.dot(left[b], weight, preferred_element_type=jnp.float32).astype(jnp.bfloat16)
+            for g in range(depth // 2):
+                for e in range(2):
+                    mid[b, pl.ds((2 * pair + e) * VB, VB), g * LANES:(g + 1) * LANES] = (
+                        part[g * VB:(g + 1) * VB, e * LANES:(e + 1) * LANES])
+            for step in beside[pair * each:(pair + 1) * each]:
+                step()
         total = lax.dot_general(
             mid[b], right[b], (((1,), (1,)), ((), ())), preferred_element_type=jnp.float32)
         total = total.reshape(rows, 2, HALF, LANES)
@@ -246,9 +245,9 @@
         for r in range(reps):
             cyc[k, r] = terms[r * share:(r + 1) * share]
 
-    weight[...] = jnp.zeros_like(weight)
     loads[5].wait()
-    prepare(0, own_tags[0])
+    for step in prepare(0, own_tags[0]):
+        step()
 
     @pl.loop(1, peers)
     def _(o):
@@ -271,8 +270,7 @@
         def _():
             x_copy(s0).wait_recv()
 
-        compute(0, s0)
-        prepare(1, tag1)
+        compute(0, s0, prepare(1, tag1))
         exchange(s0)
 
         @pl.when(n > 0)
@@ -283,8 +281,7 @@
         def _():
             x_copy(s1).wait_recv()
 
-        compute(1, s1)
-        prepare(0, tag2)
+        compute(1, s1, prepare(0, tag2))
         exchange(s1)
 
         @pl.when(n > 0)
@@ -328,7 +325,6 @@
         owned, _, depth, _ = ladder_factors.shape
         share = rows // reps
         slots = peers * CAP
-        groups = depth // QG
         bf16, f32, dma = jnp.bfloat16, jnp.float32, pltpu.SemaphoreType.DMA
         smem, vmem = pltpu.SMEM, pltpu.VMEM
         return pl.pallas_call(
@@ -352,9 +348,8 @@
                 vmem((peers, 8, LANES), jnp.int32),
                 vmem((peers, 8, LANES), jnp.int32),
                 smem((peers, 8, LANES), jnp.int32),
-                vmem((2, groups * VB, QG * VB), bf16),
+                vmem((2, depth // 2 * VB, LANES), bf16),
                 vmem((2, LANES, depth * VB), bf16),
-                vmem((2, rows, QG * VB, QG * VB), bf16),
                 vmem((2, rows * VB, depth * VB), bf16),
                 vmem((slots, reps, share * HALF, LANES), f32),
                 vmem((slots, reps - 1, share * HALF, LANES), bf16),

time: 28.2 us -> 28.1 us (level)
  no operation moved by 1% of the time
where the time goes in v3:
time: 28.1 us; the launch traced here: 27.9 us
  Pallas kernels  26.3 us (94%)
  local copies, waits for them, and re-layouts  1.61 us (6%)
    pallas_call x1, Pallas kernels, local(): pl.pallas_call(functools.partial(kernel, peers, reps, tiles, depth, share...  26.3 us
    unnamed x1, local copies, waits for them, and re-layouts  1.61 us

profile of v3, /device:TPU:0, one launch (start us, length us, event | category | flops | bytes accessed | tf_op | source)
XLA Modules:
  0.0 27.9 jit_solution(6211659074328005194)
XLA Ops:
  0.0 26.3 %ladder.1 = bf16[4,4,4096]{2,1,0:T(4,128)(2,1)} custom-call(s32[2,4]{1,0:T(2,128)} %bitcast.3, s32[4]{0:T(128)} %live_hbm.1, s32[32]{0:T(128)} %owner_hbm.1, bf16[4,8,4096]{2,1,0:T(8,128)(2,1)} %amp_hbm.1, bf16[8,8,64]{2,1,0:T(8,128)(2,1)} %bitcast.2, bf16[8,2,16,4096]{3,2,1,0:T(8,128)(2,1)} %fac_hbm.1), custom_call_target="tpu_custom_call" | custom-call | tf_op jit(solution)/shard_map/ladder/pallas_call | solution.py:330
  26.3 1.6 %copy.8 = bf16[4,4,4096]{2,1,0:T(4,128)(2,1)} copy(bf16[4,4,4096]{2,1,0:T(4,128)(2,1)} %ladder.1) | data formatting | bytes 262144

commit v4 on v3

--- a/solution.py
+++ b/solution.py
@@ -39,7 +39,7 @@
     peers, reps, tiles, depth, share, rows,
     blocks_hbm, live_hbm, owner_hbm, amp_hbm, coup_hbm, fac_hbm,
     out_ref,
-    blocks_ref, live_ref, owner_ref, amp_ref, coup_ref, fac, wide, cwide, ctile, packed, xs, xr,
+    blocks_ref, live_ref, owner_ref, amp_ref, coup_ref, fac, wide, cwide, xtile, ctile, packed, xs, xr,
     tag_send, tag_recv, tag_smem, left, right, mid, kept, rs_send, rs_recv, back, ret, cyc,
     in_sem, tag_local, tag_ssem, tag_rsem, x_ssem, x_rsem, rs_ssem, rs_rsem, b_ssem, b_rsem,
 ):
@@ -104,19 +104,19 @@
 
     loads[0].wait()
 
-    @pl.loop(0, tiles)
-    def _(k):
-        live = live_ref[k]
-        row = lax.broadcasted_iota(jnp.int32, (rows, VB * VB), 0)
-        masked = jnp.where(row < live, amp_ref[k].astype(jnp.float32), 0.0)
-        spread_rows(masked, wide)
+    row = lax.broadcasted_iota(jnp.int32, (rows, VB * VB), 0)
+    for k in range(tiles):
+        masked = jnp.where(row < live_ref[k], amp_ref[k].astype(jnp.float32), 0.0)
+        spread_rows(masked, wide.at[k])
+    for k in range(tiles):
         for pair in range(rows // 2):
-            first = wide[pl.ds(2 * pair, HALF, stride=rows), :]
-            second = wide[pl.ds(2 * pair + 1, HALF, stride=rows), :]
+            first = wide[k, pl.ds(2 * pair, HALF, stride=rows), :]
+            second = wide[k, pl.ds(2 * pair + 1, HALF, stride=rows), :]
             even, odd = pair_rows(first, second)
-            ctile[pl.ds(pair * VB, HALF, stride=2), :] = even
-            ctile[pl.ds(pair * VB + 1, HALF, stride=2), :] = odd
-        packed[k] = ctile[...].astype(jnp.bfloat16)
+            xtile[k, pl.ds(pair * VB, HALF, stride=2), :] = even
+            xtile[k, pl.ds(pair * VB + 1, HALF, stride=2), :] = odd
+    for k in range(tiles):
+        packed[k] = xtile[k].astype(jnp.bfloat16)
 
     own_tags = []
     for j in range(CAP):
@@ -164,8 +164,11 @@
     def _(o):
         tag_copy(o).start()
 
-    @pl.loop(CAP, slots)
+    @pl.loop(2 * CAP, slots)
     def _(s):
+        x_copy(s).start()
+
+    for s in range(CAP, 2 * CAP):
         x_copy(s).start()
 
     low = low_half(VB)
@@ -232,18 +235,15 @@
         back_copy(s).start()
 
     loads[4].wait()
-
-    @pl.loop(0, tiles)
-    def _(k):
-        live = live_ref[k]
-        row = lax.broadcasted_iota(jnp.int32, (rows, VB * VB), 0)
-        masked = jnp.where(row < live, amp_ref[k].astype(jnp.float32), 0.0).astype(jnp.bfloat16)
-        coup = coup_ref[...].astype(jnp.float32)
-        chosen = lax.broadcasted_iota(jnp.int32, coup.shape, 2) == blocks_ref[0, k]
-        coup = jnp.sum(jnp.where(chosen, coup, 0.0), axis=2).astype(jnp.bfloat16)
-        terms = jnp.dot(coup, masked, preferred_element_type=jnp.float32)
-        for r in range(reps):
-            cyc[k, r] = terms[r * share:(r + 1) * share]
+    for k in range(tiles):
+        for r in range(share):
+            coup = coup_ref[my_rep * share + r].astype(jnp.float32)
+            chosen = lax.broadcasted_iota(jnp.int32, coup.shape, 1) == blocks_ref[0, k]
+            coup = jnp.sum(jnp.where(chosen, coup, 0.0), axis=1, keepdims=True)
+            terms = jnp.zeros((HALF, LANES), jnp.float32)
+            for p in range(rows):
+                terms = terms + coup[p:p + 1] * wide[k, pl.ds(p, HALF, stride=rows), :]
+            cyc[k, pl.ds(r * HALF, HALF), :] = terms
 
     loads[5].wait()
     for step in prepare(0, own_tags[0]):
@@ -296,10 +296,10 @@
         back_copy(s).wait_recv()
 
     for k in range(tiles):
-        wide[pl.ds(0, share * HALF), :] = ret[slot[k]].astype(jnp.float32)
-        mine = cyc[k, my_rep]
+        wide[k, pl.ds(0, share * HALF), :] = ret[slot[k]].astype(jnp.float32) + cyc[k]
+    for k in range(tiles):
         for j in range(HALF):
-            part = wide[pl.ds(j, share, stride=HALF), :] + mine[:, j * LANES:(j + 1) * LANES]
+            part = wide[k, pl.ds(j, share, stride=HALF), :]
             out_ref[k, :, j * LANES:(j + 1) * LANES] = part.astype(out_ref.dtype)
 
     @pl.loop(1, peers)
@@ -339,9 +339,10 @@
                 vmem(amplitudes.shape, bf16),
                 vmem((rows, rows, cycle_coupling.shape[0]), bf16),
                 vmem(ladder_factors.shape, bf16),
-                vmem((rows * HALF, LANES), f32),
+                vmem((tiles, rows * HALF, LANES), f32),
                 vmem((4, depth * HALF, LANES), f32),
-                vmem((rows // 2 * VB, LANES), f32),
+                vmem((tiles, rows // 2 * VB, LANES), f32),
+                vmem((4 * VB, LANES), f32),
                 vmem((tiles, rows // 2 * VB, LANES), bf16),
                 vmem((slots, rows // 2 * VB, LANES), bf16),
                 vmem((slots, rows // 2 * VB, LANES), bf16),
@@ -356,7 +357,7 @@
                 vmem((slots, reps - 1, share * HALF, LANES), bf16),
                 vmem((slots, share * HALF, LANES), bf16),
                 vmem((slots, share * HALF, LANES), bf16),
-                vmem((tiles, reps, share, cells), f32),
+                vmem((tiles, share * HALF, LANES), f32),
                 dma((6,)),
                 dma((peers,)),
                 dma((peers,)),

time: 28.1 us -> 28.1 us (level)
  no operation moved by 1% of the time
where the time goes in v4:
time: 28.1 us; the launch traced here: 27.9 us
  Pallas kernels  26.3 us (94%)
  local copies, waits for them, and re-layouts  1.61 us (6%)
    pallas_call x1, Pallas kernels, local(): pl.pallas_call(functools.partial(kernel, peers, reps, tiles, depth, share...  26.3 us
    unnamed x1, local copies, waits for them, and re-layouts  1.61 us

profile of v4, /device:TPU:0, one launch (start us, length us, event | category | flops | bytes accessed | tf_op | source)
XLA Modules:
  0.0 27.9 jit_solution(8943937333827740941)
XLA Ops:
  0.0 26.3 %ladder.1 = bf16[4,4,4096]{2,1,0:T(4,128)(2,1)} custom-call(s32[2,4]{1,0:T(2,128)} %bitcast.3, s32[4]{0:T(128)} %live_hbm.1, s32[32]{0:T(128)} %owner_hbm.1, bf16[4,8,4096]{2,1,0:T(8,128)(2,1)} %amp_hbm.1, bf16[8,8,64]{2,1,0:T(8,128)(2,1)} %bitcast.2, bf16[8,2,16,4096]{3,2,1,0:T(8,128)(2,1)} %fac_hbm.1), custom_call_target="tpu_custom_call" | custom-call | tf_op jit(solution)/shard_map/ladder/pallas_call | solution.py:330
  26.3 1.6 %copy.8 = bf16[4,4,4096]{2,1,0:T(4,128)(2,1)} copy(bf16[4,4,4096]{2,1,0:T(4,128)(2,1)} %ladder.1) | data formatting | bytes 262144

commit v5 on v4

--- a/solution.py
+++ b/solution.py
@@ -40,8 +40,8 @@
     blocks_hbm, live_hbm, owner_hbm, amp_hbm, coup_hbm, fac_hbm,
     out_ref,
     blocks_ref, live_ref, owner_ref, amp_ref, coup_ref, fac, wide, cwide, xtile, ctile, packed, xs, xr,
-    tag_send, tag_recv, tag_smem, left, right, mid, kept, rs_send, rs_recv, back, ret, cyc,
-    in_sem, tag_local, tag_ssem, tag_rsem, x_ssem, x_rsem, rs_ssem, rs_rsem, b_ssem, b_rsem,
+    tag_send, tag_recv, tag_smem, left, right, mid, kept, back, ret, cyc,
+    in_sem, tag_local, tag_ssem, tag_rsem, x_ssem, x_rsem, b_ssem, b_rsem,
 ):
     chips = peers // 2
     slots = peers * CAP
@@ -71,12 +71,11 @@
 
     barrier = pltpu.get_barrier_semaphore()
 
-    @pl.loop(1, peers)
-    def _(o):
-        pl.semaphore_signal(barrier, inc=1, device_id={"tile": to_peer(o)}, device_id_type=MESH)
-
-    for i in range(1, reps):
-        pl.semaphore_signal(barrier, inc=1, device_id={"rep": rep_peer(i)}, device_id_type=MESH)
+    for i in range(reps):
+        @pl.loop(0 if i else 1, peers)
+        def _(o):
+            pl.semaphore_signal(
+                barrier, inc=1, device_id={"tile": to_peer(o), "rep": rep_peer(i)}, device_id_type=MESH)
 
     for load in loads[1:4]:
         load.wait()
@@ -134,7 +133,7 @@
             xs[o * CAP + j] = packed[pick]
         tag_send[o] = tags
 
-    pl.semaphore_wait(barrier, peers - 1 + reps - 1)
+    pl.semaphore_wait(barrier, peers * reps - 1)
 
     def tag_copy(o):
         return pltpu.make_async_remote_copy(
@@ -146,16 +145,10 @@
             src_ref=xs.at[s], dst_ref=xr.at[s], send_sem=x_ssem.at[s], recv_sem=x_rsem.at[s],
             device_id={"tile": to_peer(s // CAP)}, device_id_type=MESH)
 
-    def rs_copy(s, i):
+    def back_copy(s, i):
         return pltpu.make_async_remote_copy(
-            src_ref=rs_send.at[s, i - 1], dst_ref=rs_recv.at[s, i - 1],
-            send_sem=rs_ssem.at[s, i - 1], recv_sem=rs_rsem.at[s, i - 1],
-            device_id={"rep": rep_peer(i)}, device_id_type=MESH)
-
-    def back_copy(s):
-        return pltpu.make_async_remote_copy(
-            src_ref=back.at[s], dst_ref=ret.at[s], send_sem=b_ssem.at[s], recv_sem=b_rsem.at[s],
-            device_id={"tile": from_peer(s // CAP)}, device_id_type=MESH)
+            src_ref=back.at[s, i], dst_ref=ret.at[s, i], send_sem=b_ssem.at[s, i], recv_sem=b_rsem.at[s, i],
+            device_id={"tile": from_peer(s // CAP), "rep": rep_peer(i)}, device_id_type=MESH)
 
     def to_smem(o):
         return pltpu.make_async_copy(tag_recv.at[o], tag_smem.at[o], tag_local.at[o])
@@ -218,21 +211,15 @@
         for r in range(reps):
             kept[s, r] = total[r * share:(r + 1) * share].reshape(share * HALF, LANES)
 
-    def exchange(s):
+    def send(s):
+        for i in range(reps):
+            back[s, i] = kept[s, rep_peer(i)].astype(jnp.bfloat16)
         for i in range(1, reps):
-            rs_send[s, i - 1] = kept[s, rep_peer(i)].astype(jnp.bfloat16)
-            rs_copy(s, i).start()
-
-    def summed(s):
-        total = kept[s, my_rep]
-        for i in range(1, reps):
-            rs_copy(s, i).wait_recv()
-            total = total + rs_recv[s, i - 1].astype(jnp.float32)
-        return total.astype(jnp.bfloat16)
-
-    def finish(s):
-        back[s] = summed(s)
-        back_copy(s).start()
+            back_copy(s, i).start()
+
+        @pl.when(s >= CAP)
+        def _():
+            back_copy(s, 0).start()
 
     loads[4].wait()
     for k in range(tiles):
@@ -271,32 +258,27 @@
             x_copy(s0).wait_recv()
 
         compute(0, s0, prepare(1, tag1))
-        exchange(s0)
-
-        @pl.when(n > 0)
-        def _():
-            finish(2 * n)
+        send(s0)
 
         @pl.when(n < steps - 1)
         def _():
             x_copy(s1).wait_recv()
 
         compute(1, s1, prepare(0, tag2))
-        exchange(s1)
-
-        @pl.when(n > 0)
-        def _():
-            finish(s0)
+        send(s1)
 
     for j in range(CAP):
-        ret[j] = summed(j)
+        ret[j, 0] = back[j, 0]
+        for i in range(1, reps):
+            back_copy(j, i).wait_recv()
 
     @pl.loop(CAP, slots)
     def _(s):
-        back_copy(s).wait_recv()
-
-    for k in range(tiles):
-        wide[k, pl.ds(0, share * HALF), :] = ret[slot[k]].astype(jnp.float32) + cyc[k]
+        for i in range(reps):
+            back_copy(s, i).wait_recv()
+
+    for k in range(tiles):
+        wide[k, pl.ds(0, share * HALF), :] = jnp.sum(ret[slot[k]].astype(jnp.float32), axis=0) + cyc[k]
     for k in range(tiles):
         for j in range(HALF):
             part = wide[k, pl.ds(j, share, stride=HALF), :]
@@ -309,12 +291,12 @@
     @pl.loop(CAP, slots)
     def _(s):
         x_copy(s).wait_send()
-        back_copy(s).wait_send()
+        back_copy(s, 0).wait_send()
 
     @pl.loop(0, slots)
     def _(s):
         for i in range(1, reps):
-            rs_copy(s, i).wait_send()
+            back_copy(s, i).wait_send()
 
 
 def solution(mesh):
@@ -353,10 +335,8 @@
                 vmem((2, LANES, depth * VB), bf16),
                 vmem((2, rows * VB, depth * VB), bf16),
                 vmem((slots, reps, share * HALF, LANES), f32),
-                vmem((slots, reps - 1, share * HALF, LANES), bf16),
-                vmem((slots, reps - 1, share * HALF, LANES), bf16),
-                vmem((slots, share * HALF, LANES), bf16),
-                vmem((slots, share * HALF, LANES), bf16),
+                vmem((slots, reps, share * HALF, LANES), bf16),
+                vmem((slots, reps, share * HALF, LANES), bf16),
                 vmem((tiles, share * HALF, LANES), f32),
                 dma((6,)),
                 dma((peers,)),
@@ -364,10 +344,8 @@
                 dma((peers,)),
                 dma((slots,)),
                 dma((slots,)),
-                dma((slots, reps - 1)),
-                dma((slots, reps - 1)),
-                dma((slots,)),
-                dma((slots,)),
+                dma((slots, reps)),
+                dma((slots, reps)),
             ],
             compiler_params=pltpu.CompilerParams(
                 collective_id=0, has_side_effects=True, vmem_limit_bytes=62 * 2**20

time: 28.1 us -> 23 us (0.82)
  Pallas kernels: 26.3 us -> 21.2 us
    pallas_call x1, Pallas kernels: 26.3 us -> 21.2 us  [local(): pl.pallas_call(functools.partial(kernel, peers, reps, tiles, depth, share...]
where the time goes in v5:
time: 23 us; the launch traced here: 22.8 us
  Pallas kernels  21.2 us (92%)
  local copies, waits for them, and re-layouts  1.61 us (7%)
    pallas_call x1, Pallas kernels, local(): pl.pallas_call(functools.partial(kernel, peers, reps, tiles, depth, share...  21.2 us
    unnamed x1, local copies, waits for them, and re-layouts  1.61 us

profile of v5, /device:TPU:0, one launch (start us, length us, event | category | flops | bytes accessed | tf_op | source)
XLA Modules:
  0.0 22.8 jit_solution(2182949907103824762)
XLA Ops:
  0.0 21.2 %ladder.1 = bf16[4,4,4096]{2,1,0:T(4,128)(2,1)} custom-call(s32[2,4]{1,0:T(2,128)} %bitcast.3, s32[4]{0:T(128)} %live_hbm.1, s32[32]{0:T(128)} %owner_hbm.1, bf16[4,8,4096]{2,1,0:T(8,128)(2,1)} %amp_hbm.1, bf16[8,8,64]{2,1,0:T(8,128)(2,1)} %bitcast.2, bf16[8,2,16,4096]{3,2,1,0:T(8,128)(2,1)} %fac_hbm.1), custom_call_target="tpu_custom_call" | custom-call | tf_op jit(solution)/shard_map/ladder/pallas_call | solution.py:312
  21.2 1.6 %copy.8 = bf16[4,4,4096]{2,1,0:T(4,128)(2,1)} copy(bf16[4,4,4096]{2,1,0:T(4,128)(2,1)} %ladder.1) | data formatting | bytes 262144
